TPU v7x, 256 devices: a whole 4x4x8 slice. The times are simulated.
256 devices in a mesh: row: 4 (over y), col: 16 (over x, z_lo), depth: 4 (over z_hi, core).
Axes of the slice: x: 4, y: 4, z: 8 (z_hi: 2, z_lo: 4; z = z_hi * 4 + z_lo), core: 2. Of those that a mesh axis runs over, the one named last changes fastest.
Arguments:
- images: bfloat16 [4096, 1536], P(('row', 'col'), 'depth'), may hold values from -1.5 to 1.5
- texts: bfloat16 [24576, 1536], P(('row', 'col'), 'depth'), may hold values from -1.5 to 1.5
- image_potential: float32 [4096], P(('row', 'col')), may hold values from -1.75 to 0.75
- text_potential: float32 [24576], P(('row', 'col')), may hold values from -1.75 to 0.75
Outputs:
- grad_images: float32 [4096, 1536], P(('row', 'col'), 'depth')
- grad_texts: float32 [24576, 1536], P(('row', 'col'), 'depth')
All inputs are finite; a program needn't handle non-finite values.
Results may differ from a plain program's by a relative error of at most 0.015.
Values may be sent and summed in bfloat16 or wider, within the bound.
A program may use at most 64 MiB of HBM per device.

v0:
```python
import jax
import jax.numpy as jnp
from jax import lax
from jax.sharding import PartitionSpec as P

INV_TEMP = 0.4
LOSS_SCALE = 16.0


def on_device(images, texts, image_potential, text_potential):
    image_rows, image_shift = (
        lax.all_gather(images, "col", axis=0, tiled=True),
        lax.all_gather(image_potential.astype(jnp.bfloat16), "col", axis=0, tiled=True).astype(
            image_potential.dtype
        ),
    )
    text_rows, text_shift = (
        lax.all_gather(texts, "row", axis=0, tiled=True),
        lax.all_gather(text_potential.astype(jnp.bfloat16), "row", axis=0, tiled=True).astype(
            text_potential.dtype
        ),
    )
    texts_total = texts.shape[0] * lax.axis_size("row") * lax.axis_size("col")
    images_total = images.shape[0] * lax.axis_size("row") * lax.axis_size("col")
    total_rows = image_rows.shape[0]
    block_rows = min(512, total_rows)
    text_total = jnp.zeros((text_rows.shape[0], text_rows.shape[1]), jnp.float32)
    image_pieces = []
    for step_index in range(total_rows // block_rows):
        image_block = image_rows[step_index * block_rows : (step_index + 1) * block_rows]
        shift_block = image_shift[step_index * block_rows : (step_index + 1) * block_rows]
        partial_scores = jnp.dot(image_block, text_rows.T, preferred_element_type=jnp.float32)
        scores = lax.psum(partial_scores, "depth")
        transport = jnp.exp(scores * INV_TEMP + shift_block[:, None] + text_shift[None, :]).astype(
            jnp.bfloat16
        )
        image_pieces.append(jnp.dot(transport, text_rows, preferred_element_type=jnp.float32))
        text_total = text_total + jnp.dot(
            transport.T, image_block, preferred_element_type=jnp.float32
        )
    image_terms = jnp.concatenate(image_pieces, axis=0)
    grad_images = lax.psum_scatter(image_terms, "col", scatter_dimension=0, tiled=True) * (
        -LOSS_SCALE / texts_total
    )
    grad_texts = lax.psum_scatter(text_total, "row", scatter_dimension=0, tiled=True) * (
        -LOSS_SCALE / images_total
    )
    return (grad_images, grad_texts)


def solution(mesh):
    placed = (
        P(("row", "col"), "depth"),
        P(("row", "col"), "depth"),
        P(("row", "col")),
        P(("row", "col")),
    )
    return jax.shard_map(
        on_device,
        mesh=mesh,
        in_specs=placed,
        out_specs=(P(("row", "col"), "depth"), P(("row", "col"), "depth")),
        check_vma=False,
    )
```

profile of v0, /device:TPU:1, one launch (start us, length us, event | category | flops | bytes accessed | tf_op | source)
XLA Modules:
  0.0 435.8 jit_solution(10316060528205508616)
XLA Ops:
  7.2 0.0 all-gather.3.cloned.1.call-start
  7.2 0.7 all-gather.3.cloned.1.call-update
  7.9 0.0 all-reduce.4.cloned.1.call-start
  7.9 44.3 %all_gather.12 = bf16[1024,384]{1,0:T(8,128)(2,1)S(1)} all-gather(bf16[64,384]{1,0:T(8,128)(2,1)} %param.4), channel_id=1, replica_groups=mesh['row'=4,'col'=16,'depth'=4] {'col'}, dimensions={0}, use_global_device_ids=true | all-gather | bytes 835584 | tf_op jit(solution)/shard_map/all_gather | solution.py:12
  52.2 4.1 fusion.1
  56.3 0.0 copy-done
  56.3 2.7 fusion.5
  59.0 0.0 all-reduce.4.cloned.1.call-update
  59.0 0.0 reduce-scatter.3.cloned.1.call-start
  59.1 0.6 copy-done.3
  59.7 8.2 %all-gather = bf16[4,1,384]{2,1,0:T(2,128)(2,1)S(1)} all-gather(bf16[1,1,384]{2,1,0:T(2,128)(2,1)S(1)} %reshape.10), channel_id=1, replica_groups=mesh['row'=4,'col'=16,'depth'=4] {'row'}, dimensions={0}, use_global_device_ids=true | all-gather | bytes 3840 | tf_op jit(solution)/shard_map/all_gather | solution.py:19
  67.9 0.0 copy-done.4
  68.0 0.0 copy-done.5
  68.0 0.6 dynamic-slice
  69.2 0.2 dynamic-update-slice
  69.4 38.5 %all-reduce = bf16[1024]{0:T(1024)(128)(2,1)S(1)} all-reduce(bf16[1024]{0:T(1024)(128)(2,1)S(1)} %dynamic-update-slice), channel_id=1, replica_groups=mesh['row'=4,'col'=16,'depth'=4] {'col'}, use_global_device_ids=true, to_apply=%add | all-reduce | flops 1024 | bytes 4096
  107.9 195.9 %all-reduce.4.cloned.1.call-done = (f32[512,1536]{1,0:T(8,128)}, f32[512,1536]{1,0:T(8,128)}) async-done(((f32[512,1536]{1,0:T(8,128)}, f32[512,1536]{1,0:T(8,128)}), (f32[512,1536]{1,0:T(8,128)}, f32[512,1536]{1,0:T(8,128)})) %all-reduce.4.cloned.1.call-update) | async-done | bytes 6291472 | tf_op jit(solution)/shard_map/psum | solution.py:33
  303.8 3.1 fusion.7
  306.9 0.0 copy-done.1
  306.9 1.1 fusion.8
  308.0 1.3 pad_maximum_fusion
  309.3 0.0 reduce-scatter.3.cloned.1.call-update
  309.3 0.0 reduce-scatter.5.cloned.1.call-start
  309.3 0.0 copy-start.2
  309.3 3.2 fusion.3
  312.5 0.0 copy-done.2
  312.6 2.6 convolution_add_fusion
  315.2 0.0 reduce-scatter.5.cloned.1.call-update
  315.2 68.5 %reduce-scatter.3.cloned.1.call-done = f32[64,384]{1,0:T(8,128)} async-done(((f32[1024,384]{1,0:T(8,128)}), f32[64,384]{1,0:T(8,128)}) %reduce-scatter.3.cloned.1.call-update) | async-done | bytes 98320 | tf_op jit(solution)/shard_map/reduce_scatter | solution.py:42
  383.8 1.5 broadcast_multiply_fusion.1
  385.3 42.0 %reduce-scatter.5.cloned.1.call-done = f32[384,384]{1,0:T(8,128)} async-done(((f32[1536,384]{1,0:T(8,128)}), f32[384,384]{1,0:T(8,128)}) %reduce-scatter.5.cloned.1.call-update) | async-done | bytes 589840 | tf_op jit(solution)/shard_map/reduce_scatter | solution.py:45
  427.3 1.9 broadcast_multiply_fusion
  (13 shorter events, 0.1 us)
Async XLA Ops:
  7.2 45.1 %all-gather.3.cloned.1.call-start = ((), (), s32[]{:S(2)}) async-start(), calls=%async_computation.2 | async-start | bytes 1474560 | tf_op jit(solution)/shard_map/all_gather | solution.py:18
  7.9 295.9 %all-reduce.4.cloned.1.call-start = ((), (), s32[]{:S(2)}) async-start(), calls=%async_computation.5 | async-start | bytes 12582912 | tf_op jit(solution)/shard_map/psum | solution.py:33
  52.2 4.1 copy-start
  59.0 0.7 copy-start.3
  59.0 8.9 %copy-start.4 = (f32[64]{0:T(128)S(1)}, f32[64]{0:T(128)}, u32[]{:S(2)}) copy-start(f32[64]{0:T(128)} %param.6) | copy-start | bytes 772
  59.0 9.0 %copy-start.5 = (u32[256]{0:T(256)S(1)}, u32[256]{0:T(256)}, u32[]{:S(2)}) copy-start(u32[256]{0:T(256)} %constant.8) | copy-start | bytes 3076
  59.0 324.7 %reduce-scatter.3.cloned.1.call-start = ((), (), s32[]{:S(2)}) async-start(), calls=%async_computation.3 | async-start | bytes 1671168 | tf_op jit(solution)/shard_map/reduce_scatter | solution.py:42
  303.8 3.1 copy-start.1
  309.3 118.0 %reduce-scatter.5.cloned.1.call-start = ((), (), s32[]{:S(2)}) async-start(), calls=%async_computation.4 | async-start | bytes 2949120 | tf_op jit(solution)/shard_map/reduce_scatter | solution.py:45
  309.3 3.2 copy-start.2
Sparse Core Ops, SparseCore 0:
  9.8 29.8 all-gather.2
  59.1 244.6 all-reduce.3
  309.4 74.3 reduce-scatter.2
  386.3 40.9 reduce-scatter.4
where the time goes:
time: 436 us
  waiting for transfers between devices  307 us (70%)
  blocking collectives  91 us (21%)
  matrix products  16.7 us (4%)
  between operations  14.5 us (3%)
  other arithmetic  4.74 us (1%)
    psum x1, waiting for transfers between devices, on_device(): scores = lax.psum(partial_scores, 'depth')  196 us
    reduce_scatter x1, waiting for transfers between devices, on_device(): lax.psum_scatter(image_terms, 'col', scatter_dimension=0, tiled=True)  68.5 us
    all_gather x1, blocking collectives, on_device(): lax.all_gather(images, 'col', axis=0, tiled=True)  44.3 us
    reduce_scatter x1, waiting for transfers between devices, on_device(): lax.psum_scatter(text_total, 'row', scatter_dimension=0, tiled=True)  42 us
    unnamed x1, blocking collectives  38.5 us
  transfers between devices with their start and end apart: 4, of which 3 were waited for; matrix products, arithmetic and copies ran while one was open for 2% of the time, Pallas kernels for 0%

commit v1 on v0

v1 whole, which is shorter than its diff:
```python
import functools

import jax
import jax.numpy as jnp
from jax import lax
from jax.experimental import pallas as pl
from jax.experimental.pallas import tpu as pltpu
from jax.sharding import PartitionSpec as P

INV_TEMP = 0.4
LOSS_SCALE = 16.0
MESH = pl.DeviceIdType.MESH
F32, BF16 = jnp.float32, jnp.bfloat16
ZORDER = (0, 1, 7, 2, 6, 3, 5, 4)
RING = (1, 3, 2)
W = 384


def dev(x, y, z, c):
    return (y, x * 4 + z % 4, (z // 4) * 2 + c)


def cols(q, n=W):
    return pl.ds(pl.multiple_of(q * W, W), n)


def kernel(
    img_in, txt_in, ip_in, tp_in, gi_out, gt_out,
    img, txt, plan, ap, aps, tp,
    gi_own, gi_send, gi_recv, gz_send, gz_recv,
    gt_own, gx_send, gx_recv, gy_send, gy_recv, gf_send, gf_recv,
    loc_sem, yn_s, yn_r, ye_s, ye_r, ex_s, ex_r, ch_s, ch_r, iz_s, iz_r, ix_s, ix_r,
    tp_s, tp_r, ap_s, ap_r, aps_s, aps_r,
    gi_s, gi_r, gz_s, gz_r, gx_s, gx_r, gy_s, gy_r, gf_s, gf_r,
):
    y = lax.axis_index("row")
    col = lax.axis_index("col")
    d = lax.axis_index("depth")
    x, zl, h, c = col // 4, col % 4, d // 2, d % 2
    z = h * 4 + zl
    o = 1 - c
    q = 2 * h + c

    def rc(src, dst, ss, rs, target):
        return pltpu.make_async_remote_copy(
            src_ref=src, dst_ref=dst, send_sem=ss, recv_sem=rs, device_id=target, device_id_type=MESH
        )

    me_o = dev(x, y, z, o)
    bar = pltpu.get_barrier_semaphore()
    partners = [me_o]
    partners += [dev((x + k) % 4, y, z, c) for k in RING]
    partners += [dev(x, (y + k) % 4, z, c) for k in RING]
    partners += [dev(x, y, (z + k) % 8, cc) for k in ZORDER[1:] for cc in (0, 1)]
    for p in partners:
        pl.semaphore_signal(bar, inc=1, device_id=p, device_id_type=MESH)
    aps[x] = ip_in[...]
    tp[y] = tp_in[...]
    pl.semaphore_wait(bar, len(partners))

    sends = []

    def go(cp):
        cp.start()
        sends.append(cp)

    mine = txt_in.at[pl.ds(h * 2, 2)]
    for k in RING:
        go(rc(mine, txt.at[:, y, :, cols(q)], yn_s.at[k], yn_r.at[y], dev(x, (y + k) % 4, z, c)))
    go(rc(txt_in.at[pl.ds((1 - h) * 2, 2)], txt.at[:, y, :, cols(q)], ex_s.at[0], ex_r.at[0], dev(x, y, (z + 4) % 8, c)))
    loc_t = pltpu.make_async_copy(mine, txt.at[:, y, :, cols(q)], loc_sem.at[0])
    loc_t.start()
    rows_here = pl.ds(pl.multiple_of(zl * 32, 32), 32)
    for j, k in enumerate(ZORDER[1:]):
        for r in (0, 1):
            go(rc(img_in.at[pl.ds(r * 32, 32)], img.at[x, rows_here, cols(q)], iz_s.at[2 * k + r],
                  iz_r.at[2 * z + c], dev(x, y, (z + k) % 8, r)))
    go(rc(img_in.at[pl.ds(pl.multiple_of(o * 32, 32), 32)], img.at[x, rows_here, cols(q)], iz_s.at[0],
          iz_r.at[2 * z + c], me_o))
    loc_i = pltpu.make_async_copy(
        img_in.at[pl.ds(pl.multiple_of(c * 32, 32), 32)], img.at[x, rows_here, cols(q)], loc_sem.at[1])
    loc_i.start()
    go(rc(mine, txt.at[:, y, :, cols(q)], ch_s.at[0], ch_r.at[2 * y + h], me_o))
    for k in RING:
        go(rc(tp.at[y], tp.at[y], tp_s.at[k], tp_r.at[y], dev(x, (y + k) % 4, z, c)))
        go(rc(aps.at[x], ap.at[zl], ap_s.at[k], ap_r.at[zl], dev(x, y, h * 4 + (zl + k) % 4, c)))
    loc_t.wait()
    loc_i.wait()

    def piece(xx, zz):
        return img.at[xx, pl.ds(pl.multiple_of((zz % 4) * 32, 32), 32), cols(2 * (zz // 4), 2 * W)]

    def wait_iz(zz, cc):
        dst = img.at[x, pl.ds(pl.multiple_of((zz % 4) * 32, 32), 32), cols(2 * (zz // 4) + cc)]
        rc(dst, dst, iz_s.at[0], iz_r.at[2 * zz + cc], me_o).wait_recv()

    def wait_txt(sem, yy, qq):
        dst = txt.at[:, yy, :, cols(qq)]
        rc(dst, dst, yn_s.at[0], sem, me_o).wait_recv()

    qp = 2 * (1 - h) + c
    for j, k in enumerate(ZORDER):
        zz = (z + k) % 8
        if k == 0:
            wait_iz(z, o)
        else:
            wait_iz(zz, 0)
            wait_iz(zz, 1)
        for kx in RING:
            go(rc(piece(x, zz), piece(x, zz), ix_s.at[8 * kx + k], ix_r.at[8 * x + zz], dev((x + kx) % 4, y, z, c)))
        if j == 2:
            for ky in RING[:2]:
                yy = (y + ky) % 4
                wait_txt(yn_r.at[yy], yy, q)
                go(rc(txt.at[:, yy, :, cols(q)], txt.at[:, yy, :, cols(q)], ch_s.at[2 * ky], ch_r.at[2 * yy + h], me_o))
        if j == 4:
            wait_txt(ex_r.at[0], y, qp)
            for ky in RING:
                go(rc(txt.at[:, y, :, cols(qp)], txt.at[:, y, :, cols(qp)], ye_s.at[ky], ye_r.at[y],
                      dev(x, (y + ky) % 4, z, c)))
            go(rc(txt.at[:, y, :, cols(qp)], txt.at[:, y, :, cols(qp)], ch_s.at[1], ch_r.at[2 * y + 1 - h], me_o))
            yy = (y + 2) % 4
            wait_txt(yn_r.at[yy], yy, q)
            go(rc(txt.at[:, yy, :, cols(q)], txt.at[:, yy, :, cols(q)], ch_s.at[4], ch_r.at[2 * yy + h], me_o))

    asum = aps[x]
    for k in RING:
        zz = (zl + k) % 4
        rc(ap.at[zz], ap.at[zz], ap_s.at[0], ap_r.at[zz], me_o).wait_recv()
        asum = asum + ap[zz]
    ap[zl] = asum
    for kx in RING:
        go(rc(ap.at[zl], aps.at[x], aps_s.at[kx], aps_r.at[x], dev((x + kx) % 4, y, z, c)))

    for ky in RING:
        yy = (y + ky) % 4
        wait_txt(ye_r.at[yy], yy, qp)
        go(rc(txt.at[:, yy, :, cols(qp)], txt.at[:, yy, :, cols(qp)], ch_s.at[2 * ky + 1], ch_r.at[2 * yy + 1 - h], me_o))
    tsum = tp[y]
    for ky in RING:
        yy = (y + ky) % 4
        rc(tp.at[yy], tp.at[yy], tp_s.at[0], tp_r.at[yy], me_o).wait_recv()
        tsum = tsum + tp[yy]
    b = tsum[0:1]
    for ky in (0,) + RING:
        yy = (y + ky) % 4
        wait_txt(ch_r.at[2 * yy + h], yy, 2 * h + o)
        wait_txt(ch_r.at[2 * yy + 1 - h], yy, 2 * (1 - h) + o)

    texts = txt[...].reshape(768, 4 * W)
    for i, k in enumerate((0,) + RING):
        xx = (x + k) % 4
        if k == 0:
            a = asum[0:1]
        else:
            for kz in ZORDER:
                zz = (z + kz) % 8
                rc(piece(xx, zz), piece(xx, zz), ix_s.at[0], ix_r.at[8 * xx + zz], me_o).wait_recv()
            rc(aps.at[xx], aps.at[xx], aps_s.at[0], aps_r.at[xx], me_o).wait_recv()
            a = aps[xx][0:1]
        a = jnp.broadcast_to(a, (128, 128)).T
        s = lax.dot_general(img[xx], texts, (((1,), (1,)), ((), ())), preferred_element_type=F32)
        p = jnp.exp(s * INV_TEMP + jnp.concatenate([a] * 6, axis=1) + b).astype(BF16)
        plan[xx] = p
        g = jnp.dot(p, texts, preferred_element_type=F32) * (-LOSS_SCALE / 24576)
        if k == 0:
            gi_own[...] = g
        else:
            gi_send[i - 1] = g.astype(BF16)
            for zz in range(4):
                part = pl.ds(zz * 32, 32)
                go(rc(gi_send.at[i - 1, part], gi_recv.at[k - 1, part], gi_s.at[4 * k + zz], gi_r.at[4 * k + zz],
                      dev(xx, y, z, c)))

    images = img[...].reshape(512, 4 * W)

    def text_terms(half):
        p = plan[:, :, pl.ds(pl.multiple_of(half * W, W), W)].reshape(512, W)
        return lax.dot_general(p, images, (((0,), (0,)), ((), ())), preferred_element_type=F32) * (-LOSS_SCALE / 4096)

    gx_send[...] = text_terms(o).astype(BF16)
    go(rc(gx_send, gx_recv, gx_s.at[0], gx_r.at[0], me_o))
    gt_own[...] = text_terms(c)
    rc(gx_recv, gx_recv, gx_s.at[0], gx_r.at[0], me_o).wait_recv()

    for j in (0, 1):
        hh = (1 - h) if j == 0 else h
        cc = cols(2 * hh, 2 * W)
        for i, k in enumerate(RING):
            yy = (y + k) % 4
            rows = pl.ds(pl.multiple_of(yy * 96, 96), 96)
            gy_send[j, i] = (gt_own[rows, cc] + gx_recv[rows, cc].astype(F32)).astype(BF16)
            go(rc(gy_send.at[j, i], gy_recv.at[j, k - 1], gy_s.at[4 * j + k], gy_r.at[4 * j + k], dev(x, yy, z, c)))

    for zz in range(4):
        part = pl.ds(zz * 32, 32)
        t = gi_own[part]
        for k in RING:
            rc(gi_recv.at[k - 1, part], gi_recv.at[k - 1, part], gi_s.at[0], gi_r.at[4 * k + zz], me_o).wait_recv()
            t = t + gi_recv[k - 1, part].astype(F32)
        t = t.astype(BF16)
        for qq in range(4):
            gz_send[zz * 4 + qq] = t[:, qq * W : (qq + 1) * W]
    for k in ZORDER[1:]:
        zz = (z + k) % 8
        for cc in (0, 1):
            go(rc(gz_send.at[(zz % 4) * 4 + (zz // 4) * 2 + cc], gz_recv.at[z, c], gz_s.at[2 * k + cc],
                  gz_r.at[2 * z + c], dev(x, y, zz, cc)))
    go(rc(gz_send.at[zl * 4 + h * 2 + o], gz_recv.at[z, c], gz_s.at[0], gz_r.at[2 * z + c], me_o))
    gz_recv[z, c] = gz_send[zl * 4 + q]

    mine_y = pl.ds(pl.multiple_of(y * 96, 96), 96)
    for j in (0, 1):
        hh = (1 - h) if j == 0 else h
        cc = cols(2 * hh, 2 * W)
        t = gt_own[mine_y, cc] + gx_recv[mine_y, cc].astype(F32)
        for k in RING:
            rc(gy_recv.at[j, k - 1], gy_recv.at[j, k - 1], gy_s.at[0], gy_r.at[4 * j + k], me_o).wait_recv()
            t = t + gy_recv[j, k - 1].astype(F32)
        for cc in (0, 1):
            gf_send[j, cc] = t[:, cc * W : (cc + 1) * W].astype(BF16)
        if j == 0:
            for cc in (0, 1):
                go(rc(gf_send.at[0, cc], gf_recv.at[h * 2 + c], gf_s.at[cc], gf_r.at[h * 2 + c],
                      dev(x, y, (z + 4) % 8, cc)))
        else:
            go(rc(gf_send.at[1, o], gf_recv.at[h * 2 + c], gf_s.at[2], gf_r.at[h * 2 + c], me_o))
            gf_recv[h * 2 + c] = gf_send[1, c]

    for k in ZORDER[1:]:
        zz = (z + k) % 8
        for cc in (0, 1):
            rc(gz_recv.at[zz, cc], gz_recv.at[zz, cc], gz_s.at[0], gz_r.at[2 * zz + cc], me_o).wait_recv()
    rc(gz_recv.at[z, o], gz_recv.at[z, o], gz_s.at[0], gz_r.at[2 * z + o], me_o).wait_recv()
    for r in (0, 1):
        t = gz_recv[0, r].astype(F32)
        for zz in range(1, 8):
            t = t + gz_recv[zz, r].astype(F32)
        gi_out[r * 32 : (r + 1) * 32] = t

    for dd in (h * 2 + o, (1 - h) * 2, (1 - h) * 2 + 1):
        rc(gf_recv.at[dd], gf_recv.at[dd], gf_s.at[0], gf_r.at[dd], me_o).wait_recv()
    for dd in range(4):
        gt_out[dd * 96 : (dd + 1) * 96] = gf_recv[dd].astype(F32)

    for cp in sends:
        cp.wait_send()


def on_device(images, texts, image_potential, text_potential):
    y = lax.axis_index("row")
    zl = lax.axis_index("col") % 4
    h, c = lax.axis_index("depth") // 2, lax.axis_index("depth") % 2
    lane = lax.iota(jnp.int32, 128) // 32
    half = lax.dynamic_slice(image_potential, (c * 32,), (32,))
    ip = jnp.where(lane == zl, jnp.tile(half, 4), 0.0)
    ip = jnp.broadcast_to(ip[None], (8, 128))
    th = lax.dynamic_slice(text_potential, (h * 192,), (192,)).reshape(2, 1, 96)
    tp = jnp.where((jnp.arange(4) == y)[None, :, None], th, 0.0).reshape(1, 768)
    tp = jnp.broadcast_to(tp, (8, 768))
    dma = pltpu.SemaphoreType.DMA
    vm = pltpu.VMEM
    return pl.pallas_call(
        kernel,
        out_shape=(jax.ShapeDtypeStruct((64, W), F32), jax.ShapeDtypeStruct((384, W), F32)),
        in_specs=[
            pl.BlockSpec(memory_space=pl.ANY),
            pl.BlockSpec(memory_space=pl.ANY),
            pl.BlockSpec(memory_space=pltpu.VMEM),
            pl.BlockSpec(memory_space=pltpu.VMEM),
        ],
        out_specs=(pl.BlockSpec(memory_space=pltpu.VMEM), pl.BlockSpec(memory_space=pltpu.VMEM)),
        scratch_shapes=[
            vm((4, 128, 4 * W), BF16), vm((2, 4, 96, 4 * W), BF16), vm((4, 128, 768), BF16),
            vm((4, 8, 128), F32), vm((4, 8, 128), F32), vm((4, 8, 768), F32),
            vm((128, 4 * W), F32), vm((3, 128, 4 * W), BF16), vm((3, 128, 4 * W), BF16),
            vm((16, 32, W), BF16), vm((8, 2, 32, W), BF16),
            vm((384, 4 * W), F32), vm((384, 4 * W), BF16), vm((384, 4 * W), BF16),
            vm((2, 3, 96, 2 * W), BF16), vm((2, 3, 96, 2 * W), BF16), vm((2, 2, 96, W), BF16), vm((4, 96, W), BF16),
            dma((2,)), dma((4,)), dma((4,)), dma((4,)), dma((4,)), dma((1,)), dma((1,)), dma((8,)), dma((8,)),
            dma((16,)), dma((16,)), dma((32,)), dma((32,)),
            dma((4,)), dma((4,)), dma((4,)), dma((4,)), dma((4,)), dma((4,)),
            dma((16,)), dma((16,)), dma((16,)), dma((16,)), dma((1,)), dma((1,)), dma((8,)), dma((8,)), dma((4,)), dma((4,)),
        ],
        compiler_params=pltpu.CompilerParams(
            collective_id=0, has_side_effects=True, vmem_limit_bytes=48 * 1024 * 1024
        ),
        cost_estimate=pl.CostEstimate(flops=3623878656, bytes_accessed=2000000, transcendentals=393216),
    )(images, texts.reshape(4, 96, W), ip, tp)


def solution(mesh):
    placed = (
        P(("row", "col"), "depth"),
        P(("row", "col"), "depth"),
        P(("row", "col")),
        P(("row", "col")),
    )
    return jax.shard_map(
        on_device,
        mesh=mesh,
        in_specs=placed,
        out_specs=(P(("row", "col"), "depth"), P(("row", "col"), "depth")),
        check_vma=False,
    )
```

time: 436 us -> 83.4 us (0.19)
  waiting for transfers between devices: 307 us -> 0 us
  blocking collectives: 91 us -> 0 us
  Pallas kernels: 0 us -> 79 us
  matrix products: 16.7 us -> 0 us
  between operations: 14.5 us -> 0.73 us
  other arithmetic: 4.74 us -> 0.08 us
    psum x1 -> x0, waiting for transfers between devices: 196 us -> none  [on_device(): scores = lax.psum(partial_scores, 'depth')]
    reduce_scatter x2 -> x0, waiting for transfers between devices: 111 us -> none  [the longest x1 68.5 us: on_device(): lax.psum_scatter(image_terms, 'col', scatter_dimension=0, tiled=True)]
    pallas_call x0 -> x1, Pallas kernels: none -> 79 us  [on_device(): pl.pallas_call(kernel, out_shape=(jax.ShapeDtypeStruct((64, W), F32), jax...]
    all_gather x2 -> x0, blocking collectives: 52.5 us -> none  [the longest x1 44.3 us: on_device(): lax.all_gather(images, 'col', axis=0, tiled=True)]
    unnamed x1 -> x0, blocking collectives: 38.5 us -> none
    dot_general x6 -> x0, matrix products: 16.7 us -> none  [the longest x2 6.75 us: on_device(): jnp.dot(image_block, text_rows.T, preferred_element_type=jnp.float32)]
  transfers between devices with their start and end apart: 4 -> 0, of which waited for: 3 -> 0; matrix products, arithmetic and copies ran while one was open for 2% -> 0% of each run, Pallas kernels for 0% -> 0%
where the time goes in v1:
time: 83.4 us; the launch traced here: 83.3 us
  Pallas kernels  79 us (95%)
  local copies, waits for them, and re-layouts  3.42 us (4%)
    pallas_call x1, Pallas kernels, on_device(): pl.pallas_call(kernel, out_shape=(jax.ShapeDtypeStruct((64, W), F32), jax...  79 us
    unnamed x10, local copies, waits for them, and re-layouts  3.02 us

profile of v1, /device:TPU:1, one launch (start us, length us, event | category | flops | bytes accessed | tf_op | source)
XLA Modules:
  0.0 83.3 jit_solution(1186954133838603929)
XLA Ops:
  0.6 0.0 copy-start.3
  0.7 0.0 copy-start.2
  0.7 0.0 copy-start.1
  0.7 0.6 copy-done.3
  1.3 0.1 dynamic_slice.6
  1.4 0.0 copy-done.2
  1.4 0.1 dynamic_slice.7
  1.5 0.1 broadcast_in_dim.41
  1.5 0.1 tile.10
  1.6 0.1 broadcast_select_fusion
  1.7 0.1 select_n.57
  1.8 0.0 copy-done.1
  1.8 0.0 copy-start
  1.8 1.0 %copy-done = bf16[384,384]{1,0:T(8,128)(2,1)S(1)} copy-done((bf16[384,384]{1,0:T(8,128)(2,1)S(1)}, bf16[384,384]{1,0:T(8,128)(2,1)}, u32[]{:S(2)}) %copy-start) | copy-done | bytes 294936
  2.8 79.0 %shard_map.59 = (f32[64,384]{1,0:T(8,128)S(1)}, f32[384,384]{1,0:T(8,128)S(1)}) custom-call(bf16[64,384]{1,0:T(8,128)(2,1)S(1)} %copy-done.1, bf16[4,96,384]{2,1,0:T(8,128)(2,1)S(1)} %bitcast.1, f32[8,128]{1,0:T(8,128)S(1)} %broadcast_in_dim.39.ip_in, f32[8,768]{1,0:T(8,128)S(1)} %broadcast_in_dim.44.tp_in), custom_call_target="tpu_custom_call" | custom-call | flops 3623878656 | bytes 2000000 | tf_op jit(solution)/shard_map/pallas_call | solution.py:263
  81.8 0.6 copy.8
  82.4 0.8 copy.9
  (5 shorter events, 0.0 us)
Async XLA Ops:
  0.6 0.7 copy-start.3
  0.7 0.7 copy-start.2
  0.7 1.1 %copy-start.1 = (bf16[64,384]{1,0:T(8,128)(2,1)S(1)}, bf16[64,384]{1,0:T(8,128)(2,1)}, u32[]{:S(2)}) copy-start(bf16[64,384]{1,0:T(8,128)(2,1)} %img_in.1) | copy-start | bytes 147460
  1.8 1.0 %copy-start = (bf16[384,384]{1,0:T(8,128)(2,1)S(1)}, bf16[384,384]{1,0:T(8,128)(2,1)}, u32[]{:S(2)}) copy-start(bf16[384,384]{1,0:T(8,128)(2,1)} %param.5) | copy-start | bytes 884740

commit v2 on v0

v2 whole, which is shorter than its diff:
```python
import jax
import jax.numpy as jnp
from jax import lax
from jax.experimental import pallas as pl
from jax.experimental.pallas import tpu as pltpu
from jax.sharding import PartitionSpec as P

INV_TEMP = 0.4
LOSS_SCALE = 16.0
MESH = pl.DeviceIdType.MESH
F32, BF16 = jnp.float32, jnp.bfloat16
ZORDER = (1, 7, 2, 6, 4)
RING = (1, 3, 2)
ORDER = (0, 1, 3, 2)
W = 384


def dev(x, y, z, c):
    return (y, x * 4 + z % 4, (z // 4) * 2 + c)


def cols(q, n=W):
    return pl.ds(pl.multiple_of(q * W, W), n)


def kernel(
    img_in, txt_in, ip_in, tp_in, gi_out, gt_out,
    img, txt, plan, ipv, tpv, ap, aps, tp,
    gi_own, gi_send, gi_recv, gz_send, gz, gf, gq_recv, gr_recv,
    gt_own, gx_send, gx_recv, gy_send, gy_recv, gf_send,
    loc_sem, yn_s, yn_r, ye_s, ye_r, ex_s, ex_r, ch_s, ch_r, iz_s, iz_r, ix_s, ix_r, fw_s, fw_r,
    tp_s, tp_r, ap_s, ap_r, aps_s, aps_r,
    gi_s, gi_r, gz_s, gz_r, gr_s, gr_r, gx_s, gx_r, gy_s, gy_r, gf_s, gf_r,
):
    y = lax.axis_index("row")
    col = lax.axis_index("col")
    d = lax.axis_index("depth")
    x, zl, h, c = col // 4, col % 4, d // 2, d % 2
    z = h * 4 + zl
    o = 1 - c
    q = 2 * h + c
    qp = 2 * (1 - h) + c

    def rc(src, dst, ss, rs, target):
        return pltpu.make_async_remote_copy(
            src_ref=src, dst_ref=dst, send_sem=ss, recv_sem=rs, device_id=target, device_id_type=MESH
        )

    me_o = dev(x, y, z, o)

    def got(dst, rs):
        rc(dst, dst, yn_s.at[0], rs, me_o).wait_recv()

    bar = pltpu.get_barrier_semaphore()
    partners = [me_o]
    partners += [dev((x + k) % 4, y, z, c) for k in RING]
    partners += [dev(x, (y + k) % 4, z, c) for k in RING]
    partners += [dev(x, y, (z + k) % 8, cc) for k in ZORDER for cc in (0, 1)]
    partners += [dev(x, y, (z + k) % 8, c) for k in (3, 5)]
    for p in partners:
        pl.semaphore_signal(bar, inc=1, device_id=p, device_id_type=MESH)

    lp = [pltpu.make_async_copy(ip_in, ipv, loc_sem.at[2]), pltpu.make_async_copy(tp_in, tpv, loc_sem.at[3])]
    for cp in lp:
        cp.start()
    for cp in lp:
        cp.wait()
    lane = lax.broadcasted_iota(jnp.int32, (8, 128), 1)
    v = ipv[...].reshape(1, 64)
    v = jnp.broadcast_to(jnp.concatenate([v, v], axis=1), (8, 128))
    v = pltpu.roll(v, ((zl + 4 - c) % 4) * 32, 1)
    aps[x] = jnp.where(lane // 32 == zl, v, 0.0)
    lane = lax.broadcasted_iota(jnp.int32, (8, W), 1)
    v = jnp.broadcast_to(tpv[...].reshape(1, W), (8, W))
    for s in (0, 1):
        t = pltpu.roll(v, (y * 96 + 2 * W - h * 192 - s * 96) % W, 1)
        tp[y, :, s * W : (s + 1) * W] = jnp.where(lane // 96 == y, t, 0.0)
    pl.semaphore_wait(bar, len(partners))

    sends = []

    def go(cp):
        cp.start()
        sends.append(cp)

    def text_piece(yy, qq, s):
        return txt.at[s, yy, :, cols(qq)]

    mine = txt_in.at[pl.ds(h * 2, 2)]
    rows_here = pl.ds(pl.multiple_of(x * 32, 32), 32)
    go(rc(img_in.at[pl.ds(pl.multiple_of(o * 32, 32), 32)], img.at[zl, rows_here, cols(q)], iz_s.at[0],
          iz_r.at[2 * z + c], me_o))
    for k in (1, 7, 2, 6):
        for r in (0, 1):
            go(rc(img_in.at[pl.ds(r * 32, 32)], img.at[zl, rows_here, cols(q)], iz_s.at[2 * min(k, 8 - k) + r + (8 if k > 4 else 0)],
                  iz_r.at[2 * z + c], dev(x, y, (z + k) % 8, r)))
    for k in RING:
        go(rc(mine, txt.at[:, y, :, cols(q)], yn_s.at[k], yn_r.at[y], dev(x, (y + k) % 4, z, c)))
    for s in (0, 1):
        go(rc(txt_in.at[(1 - h) * 2 + s], text_piece(y, q, s), ex_s.at[s], ex_r.at[s], dev(x, y, (z + 4) % 8, c)))
    loc_i = pltpu.make_async_copy(
        img_in.at[pl.ds(pl.multiple_of(c * 32, 32), 32)], img.at[zl, rows_here, cols(q)], loc_sem.at[1])
    loc_i.start()
    loc_t = pltpu.make_async_copy(mine, txt.at[:, y, :, cols(q)], loc_sem.at[0])
    loc_t.start()
    go(rc(mine, txt.at[:, y, :, cols(q)], ch_s.at[0], ch_r.at[y], me_o))
    for k in RING:
        go(rc(tp.at[y], tp.at[y], tp_s.at[k], tp_r.at[y], dev(x, (y + k) % 4, z, c)))
        go(rc(aps.at[x], ap.at[zl], ap_s.at[k], ap_r.at[zl], dev(x, y, h * 4 + (zl + k) % 4, c)))
    loc_i.wait()

    def piece(xx, zz, start=0, n=32):
        return img.at[zz % 4, pl.ds(pl.multiple_of(xx * 32 + start, 16), n), cols(2 * (zz // 4), 2 * W)]

    def pass_on(k):
        zz = (z + k) % 8
        for e, kx in ((0, 1), (1, 3)):
            back = (x + 4 - kx) % 4
            got(piece(back, zz), ix_r.at[8 * back + zz])
            half = piece(back, zz, 16 * e, 16)
            go(rc(half, half, fw_s.at[2 * k + e], fw_r.at[2 * zz + e], dev((x + kx) % 4, y, z, c)))

    def along_x(k):
        zz = (z + k) % 8
        if k == 0:
            got(img.at[zl, rows_here, cols(2 * h + o)], iz_r.at[2 * z + o])
        elif k in (3, 5):
            got(piece(x, zz), iz_r.at[2 * zz])
        elif k == 4:
            for e in (0, 1):
                got(piece(x, zz, 16 * e, 16), iz_r.at[2 * zz + e])
        else:
            for cc in (0, 1):
                got(img.at[zz % 4, rows_here, cols(2 * (zz // 4) + cc)], iz_r.at[2 * zz + cc])
        if k in (2, 6):
            e, step = (1, 7) if k == 2 else (0, 1)
            p = piece(x, zz)
            go(rc(p, p, iz_s.at[6 + 2 * e], iz_r.at[2 * zz], dev(x, y, (z + step) % 8, c)))
            p = piece(x, zz, 16 * e, 16)
            go(rc(p, p, iz_s.at[7 + 2 * e], iz_r.at[2 * zz + e], dev(x, y, (z + 2 * step) % 8, c)))
        for e, kx in ((0, 1), (1, 3)):
            go(rc(piece(x, zz), piece(x, zz), ix_s.at[2 * k + e], ix_r.at[8 * x + zz], dev((x + kx) % 4, y, z, c)))

    def forward_swapped(s):
        p = text_piece(y, qp, s)
        got(p, ex_r.at[s])
        for ky in RING:
            go(rc(p, p, ye_s.at[2 * ky + s], ye_r.at[2 * y + s], dev(x, (y + ky) % 4, z, c)))
        go(rc(p, p, ch_s.at[4 + s], ch_r.at[4 + 2 * y + s], me_o))

    def to_other_core(ky):
        yy = (y + ky) % 4
        p = txt.at[:, yy, :, cols(q)]
        got(p, yn_r.at[yy])
        go(rc(p, p, ch_s.at[ky], ch_r.at[yy], me_o))

    along_x(0)
    along_x(1)
    along_x(7)
    pass_on(0)
    along_x(2)
    along_x(6)
    forward_swapped(0)
    pass_on(1)
    pass_on(7)
    along_x(3)
    along_x(5)
    forward_swapped(1)
    pass_on(2)
    pass_on(6)
    along_x(4)
    for k in RING:
        to_other_core(k)
    pass_on(3)
    pass_on(5)
    pass_on(4)

    asum = aps[x]
    for k in RING:
        zz = (zl + k) % 4
        got(ap.at[zz], ap_r.at[zz])
        asum = asum + ap[zz]
    ap[zl] = asum
    for kx in RING:
        go(rc(ap.at[zl], aps.at[x], aps_s.at[kx], aps_r.at[x], dev((x + kx) % 4, y, z, c)))

    for s in (0, 1):
        for ky in RING:
            yy = (y + ky) % 4
            p = text_piece(yy, qp, s)
            got(p, ye_r.at[2 * yy + s])
            go(rc(p, p, ch_s.at[4 + 2 * ky + s], ch_r.at[4 + 2 * yy + s], me_o))
    loc_t.wait()
    tsum = tp[y]
    for ky in RING:
        yy = (y + ky) % 4
        got(tp.at[yy], tp_r.at[yy])
        tsum = tsum + tp[yy]
    b = tsum[0:1]
    a_of = {0: jnp.broadcast_to(asum[0:1], (128, 128)).T}
    for kx in RING:
        xx = (x + kx) % 4
        got(aps.at[xx], aps_r.at[xx])
        a_of[kx] = jnp.broadcast_to(aps[xx][0:1], (128, 128)).T
    for kx in (0,) + RING:
        gi_own[0, pl.ds(pl.multiple_of(((x + kx) % 4) * 128, 128), 128), 0:128] = a_of[kx]
    for ky in (0,) + RING:
        yy = (y + ky) % 4
        got(txt.at[:, yy, :, cols(2 * h + o)], ch_r.at[yy])
        for s in (0, 1):
            got(text_piece(yy, 2 * (1 - h) + o, s), ch_r.at[4 + 2 * yy + s])

    texts = txt[...].reshape(768, 4 * W)
    for zz in range(8):
        for e in (0, 1):
            got(piece((x + 2) % 4, zz, 16 * e, 16), fw_r.at[2 * zz + e])
    for half in (0, 1):
        a = jnp.concatenate(
            [gi_own[0, pl.ds(xx * 128 + zz * 32, 32), 0:128] for zz in (2 * half, 2 * half + 1) for xx in range(4)], axis=0)
        i = img[2 * half : 2 * half + 2].reshape(256, 4 * W)
        s = lax.dot_general(i, texts, (((1,), (1,)), ((), ())), preferred_element_type=F32)
        p = jnp.exp(s * INV_TEMP + jnp.concatenate([a] * 6, axis=1) + b).astype(BF16)
        plan[2 * half : 2 * half + 2] = p.reshape(2, 128, 768)

    def own_rows(j, k, e, n=16):
        return pl.ds(pl.multiple_of(j * 128 + ((x + k) % 4) * 32 + 16 * e, 16), n)

    def image_send(j, slot, kx):
        go(rc(gi_send.at[j, slot], gi_recv.at[j, slot], gi_s.at[6 * j + slot], gi_r.at[6 * j + slot],
              dev((x + kx) % 4, y, z, c)))

    def image_terms(j):
        zj = (zl + ORDER[j]) % 4
        gi_own[1, pl.ds(j * 128, 128)] = jnp.dot(plan[zj], texts, preferred_element_type=F32) * (-LOSS_SCALE / 24576)
        for slot, (k, e, kx) in enumerate(((2, 0, 1), (2, 1, 3), (1, 1, 1), (3, 0, 3))):
            gi_send[j, slot] = gi_own[1, own_rows(j, k, e)].astype(BF16)
            image_send(j, slot, kx)

    def image_relay(j):
        for slot, (k, e) in enumerate(((1, 0), (3, 1))):
            got(gi_recv.at[j, slot], gi_r.at[6 * j + slot])
            gi_send[j, 4 + slot] = (gi_own[1, own_rows(j, k, e)] + gi_recv[j, slot].astype(F32)).astype(BF16)
            image_send(j, 4 + slot, k)

    def text_terms(half, cc):
        p = plan[:, :, pl.ds(pl.multiple_of(half * W, W), W)].reshape(512, W)
        i = img[:, :, cc].reshape(512, 2 * W)
        return lax.dot_general(p, i, (((0,), (0,)), ((), ())), preferred_element_type=F32) * (-LOSS_SCALE / 4096)

    wide = [cols(2 * (1 - h), 2 * W), cols(2 * h, 2 * W)]

    def text_other(j):
        gx_send[j] = text_terms(o, wide[j]).astype(BF16)
        go(rc(gx_send.at[j], gx_recv.at[j], gx_s.at[j], gx_r.at[j], me_o))

    def text_own(j):
        gt_own[j] = text_terms(c, wide[j])
        got(gx_recv.at[j], gx_r.at[j])
        for i, k in enumerate(RING):
            yy = (y + k) % 4
            rows = pl.ds(pl.multiple_of(yy * 96, 96), 96)
            gy_send[j, i] = (gt_own[j, rows] + gx_recv[j, rows].astype(F32)).astype(BF16)
            go(rc(gy_send.at[j, i], gy_recv.at[j, k - 1], gy_s.at[4 * j + k], gy_r.at[4 * j + k], dev(x, yy, z, c)))

    def image_sums(j):
        for slot in (2, 3, 4, 5):
            got(gi_recv.at[j, slot], gi_r.at[6 * j + slot])
        for e, slots in ((0, (3, 4)), (1, (2, 5))):
            t = gi_own[1, own_rows(j, 0, e)]
            for slot in slots:
                t = t + gi_recv[j, slot].astype(F32)
            if j < 3:
                gz_send[j, 16 * e : 16 * e + 16] = t.astype(BF16)
            else:
                gi_own[0, 16 * e : 16 * e + 16] = t
        for dz in ((0, 4), (1, 5), (7, 3), (2, 6))[j]:
            zz = (z + dz) % 8
            both = cols(2 * (zz // 4), 2 * W)
            if dz == 4:
                for e, step in ((0, 2), (1, 6)):
                    go(rc(gz_send.at[j, pl.ds(16 * e, 16), both], gq_recv.at[e], gr_s.at[e], gr_r.at[e],
                          dev(x, y, (z + step) % 8, c)))
            elif dz in (3, 5):
                e, step = (0, 1) if dz == 3 else (1, 7)
                go(rc(gz_send.at[j, :, both], gr_recv.at[e], gr_s.at[2 + e], gr_r.at[2 + e],
                      dev(x, y, (z + step) % 8, c)))
            elif dz == 0:
                go(rc(gz_send.at[0, :, cols(2 * h + o)], gz.at[z, c], gz_s.at[0], gz_r.at[2 * z + c], me_o))
                gz[z, c] = gz_send[0, :, cols(q)]
            else:
                if dz in (2, 6):
                    e = 0 if dz == 2 else 1
                    got(gq_recv.at[e], gr_r.at[e])
                    got(gr_recv.at[e], gr_r.at[2 + e])
                    for g in (0, 1):
                        t = gi_own[0, 16 * g : 16 * g + 16, both] + gr_recv[e, 16 * g : 16 * g + 16].astype(F32)
                        if g == e:
                            t = t + gq_recv[e].astype(F32)
                        gz_send[j, 16 * g : 16 * g + 16, both] = t.astype(BF16)
                for cc in (0, 1):
                    go(rc(gz_send.at[j, :, cols(2 * (zz // 4) + cc)], gz.at[z, c], gz_s.at[2 * dz + cc],
                          gz_r.at[2 * z + c], dev(x, y, zz, cc)))

    def text_sums(j):
        mine_y = pl.ds(pl.multiple_of(y * 96, 96), 96)
        t = gt_own[j, mine_y] + gx_recv[j, mine_y].astype(F32)
        for k in RING:
            got(gy_recv.at[j, k - 1], gy_r.at[4 * j + k])
            t = t + gy_recv[j, k - 1].astype(F32)
        gf_send[j] = t.astype(BF16)
        part = gf.at[h * 2 + c]
        if j == 0:
            for cc in (0, 1):
                go(rc(gf_send.at[0, :, pl.ds(cc * W, W)], part, gf_s.at[cc], gf_r.at[h * 2 + c], dev(x, y, (z + 4) % 8, cc)))
        else:
            go(rc(gf_send.at[1, :, cols(o)], part, gf_s.at[2], gf_r.at[h * 2 + c], me_o))
            gf[h * 2 + c] = gf_send[1, :, cols(c)]

    image_terms(0)
    text_other(0)
    image_terms(1)
    text_own(0)
    image_terms(2)
    text_other(1)
    image_terms(3)
    text_own(1)
    image_relay(0)
    image_relay(1)
    image_relay(2)
    image_relay(3)
    image_sums(0)
    image_sums(1)
    text_sums(0)
    image_sums(2)
    image_sums(3)
    text_sums(1)

    for k in (1, 7, 2, 6):
        zz = (z + k) % 8
        for cc in (0, 1):
            got(gz.at[zz, cc], gz_r.at[2 * zz + cc])
    got(gz.at[z, o], gz_r.at[2 * z + o])
    for dd in (h * 2 + o, (1 - h) * 2, (1 - h) * 2 + 1):
        got(gf.at[dd], gf_r.at[dd])
    for r in (0, 1):
        t = gz[z, r].astype(F32)
        for k in (1, 7, 2, 6):
            t = t + gz[(z + k) % 8, r].astype(F32)
        gi_out[r * 32 : (r + 1) * 32] = t
    for dd in range(4):
        gt_out[dd * 96 : (dd + 1) * 96] = gf[dd].astype(F32)
    for cp in sends:
        cp.wait_send()


def on_device(images, texts, image_potential, text_potential):
    dma = pltpu.SemaphoreType.DMA
    vm = pltpu.VMEM
    hbm = pl.BlockSpec(memory_space=pltpu.HBM)
    return pl.pallas_call(
        kernel,
        out_shape=(jax.ShapeDtypeStruct((64, W), F32), jax.ShapeDtypeStruct((384, W), F32)),
        in_specs=[hbm] * 4,
        out_specs=(pl.BlockSpec(memory_space=pltpu.VMEM), pl.BlockSpec(memory_space=pltpu.VMEM)),
        scratch_shapes=[
            vm((4, 128, 4 * W), BF16), vm((2, 4, 96, 4 * W), BF16), vm((4, 128, 768), BF16),
            vm((64,), F32), vm((W,), F32), vm((4, 8, 128), F32), vm((4, 8, 128), F32), vm((4, 8, 768), F32),
            vm((2, 512, 4 * W), F32), vm((4, 6, 16, 4 * W), BF16), vm((4, 6, 16, 4 * W), BF16), vm((4, 32, 4 * W), BF16),
            vm((8, 2, 32, W), BF16), vm((4, 96, W), BF16),
            vm((2, 16, 2 * W), BF16), vm((2, 32, 2 * W), BF16),
            vm((2, 384, 2 * W), F32), vm((2, 384, 2 * W), BF16), vm((2, 384, 2 * W), BF16),
            vm((2, 3, 96, 2 * W), BF16), vm((2, 3, 96, 2 * W), BF16), vm((2, 96, 2 * W), BF16),
            dma((4,)), dma((4,)), dma((4,)), dma((8,)), dma((8,)), dma((2,)), dma((2,)), dma((12,)), dma((12,)),
            dma((16,)), dma((16,)), dma((16,)), dma((32,)), dma((16,)), dma((16,)),
            dma((4,)), dma((4,)), dma((4,)), dma((4,)), dma((4,)), dma((4,)),
            dma((24,)), dma((24,)), dma((16,)), dma((16,)), dma((4,)), dma((4,)), dma((2,)), dma((2,)), dma((8,)), dma((8,)), dma((4,)), dma((4,)),
        ],
        compiler_params=pltpu.CompilerParams(
            collective_id=0, has_side_effects=True, vmem_limit_bytes=63 * 1024 * 1024
        ),
        cost_estimate=pl.CostEstimate(flops=3623878656, bytes_accessed=2000000, transcendentals=393216),
    )(images, texts.reshape(4, 96, W), image_potential, text_potential)


def solution(mesh):
    placed = (
        P(("row", "col"), "depth"),
        P(("row", "col"), "depth"),
        P(("row", "col")),
        P(("row", "col")),
    )
    return jax.shard_map(
        on_device,
        mesh=mesh,
        in_specs=placed,
        out_specs=(P(("row", "col"), "depth"), P(("row", "col"), "depth")),
        check_vma=False,
    )
```

time: 436 us -> 71.6 us (0.16)
  waiting for transfers between devices: 307 us -> 0 us
  blocking collectives: 91 us -> 0 us
  Pallas kernels: 0 us -> 67.3 us
  matrix products: 16.7 us -> 0 us
  between operations: 14.5 us -> 0.64 us
  other arithmetic: 4.74 us -> 0 us
    psum x1 -> x0, waiting for transfers between devices: 196 us -> none  [on_device(): scores = lax.psum(partial_scores, 'depth')]
    reduce_scatter x2 -> x0, waiting for transfers between devices: 111 us -> none  [the longest x1 68.5 us: on_device(): lax.psum_scatter(image_terms, 'col', scatter_dimension=0, tiled=True)]
    pallas_call x0 -> x1, Pallas kernels: none -> 67.3 us  [on_device(): pl.pallas_call(kernel, out_shape=(jax.ShapeDtypeStruct((64, W), F32), jax...]
    all_gather x2 -> x0, blocking collectives: 52.5 us -> none  [the longest x1 44.3 us: on_device(): lax.all_gather(images, 'col', axis=0, tiled=True)]
    unnamed x1 -> x0, blocking collectives: 38.5 us -> none
    dot_general x6 -> x0, matrix products: 16.7 us -> none  [the longest x2 6.75 us: on_device(): jnp.dot(image_block, text_rows.T, preferred_element_type=jnp.float32)]
  transfers between devices with their start and end apart: 4 -> 0, of which waited for: 3 -> 0; matrix products, arithmetic and copies ran while one was open for 2% -> 0% of each run, Pallas kernels for 0% -> 0%
where the time goes in v2:
time: 71.6 us; the launch traced here: 71.4 us
  Pallas kernels  67.3 us (94%)
  local copies, waits for them, and re-layouts  3.46 us (5%)
    pallas_call x1, Pallas kernels, on_device(): pl.pallas_call(kernel, out_shape=(jax.ShapeDtypeStruct((64, W), F32), jax...  67.3 us
    unnamed x2, local copies, waits for them, and re-layouts  3.46 us

profile of v2, /device:TPU:1, one launch (start us, length us, event | category | flops | bytes accessed | tf_op | source)
XLA Modules:
  0.0 71.4 jit_solution(9517520243734728460)
XLA Ops:
  0.6 67.3 %shard_map.59 = (f32[64,384]{1,0:T(8,128)}, f32[384,384]{1,0:T(8,128)}) custom-call(bf16[64,384]{1,0:T(8,128)(2,1)} %img_in.1, bf16[4,96,384]{2,1,0:T(8,128)(2,1)} %bitcast.1, f32[64]{0:T(128)} %ip_in.1, f32[384]{0:T(512)} %tp_in.1), custom_call_target="tpu_custom_call" | custom-call | flops 3623878656 | bytes 2000000 | tf_op jit(solution)/shard_map/pallas_call | solution.py:360
  67.9 1.5 %copy.8 = f32[64,384]{1,0:T(8,128)} copy(f32[64,384]{1,0:T(8,128)} %get-tuple-element.4) | data formatting | bytes 196608
  69.5 1.9 %copy.9 = f32[384,384]{1,0:T(8,128)} copy(f32[384,384]{1,0:T(8,128)} %get-tuple-element.5) | data formatting | bytes 1179648

commit v3 on v2

--- a/solution.py
+++ b/solution.py
@@ -12,6 +12,7 @@
 ZORDER = (1, 7, 2, 6, 4)
 RING = (1, 3, 2)
 ORDER = (0, 1, 3, 2)
+PAIRS = ((0, 4), (1, 5), (7, 3), (2, 6))
 W = 384
 
 
@@ -88,16 +89,29 @@
 
     mine = txt_in.at[pl.ds(h * 2, 2)]
     rows_here = pl.ds(pl.multiple_of(x * 32, 32), 32)
-    go(rc(img_in.at[pl.ds(pl.multiple_of(o * 32, 32), 32)], img.at[zl, rows_here, cols(q)], iz_s.at[0],
-          iz_r.at[2 * z + c], me_o))
-    for k in (1, 7, 2, 6):
+    mine = txt_in.at[pl.ds(h * 2, 2)]
+
+    def send_images(k):
         for r in (0, 1):
             go(rc(img_in.at[pl.ds(r * 32, 32)], img.at[zl, rows_here, cols(q)], iz_s.at[2 * min(k, 8 - k) + r + (8 if k > 4 else 0)],
                   iz_r.at[2 * z + c], dev(x, y, (z + k) % 8, r)))
-    for k in RING:
-        go(rc(mine, txt.at[:, y, :, cols(q)], yn_s.at[k], yn_r.at[y], dev(x, (y + k) % 4, z, c)))
-    for s in (0, 1):
+
+    def send_texts():
+        for k in RING:
+            go(rc(mine, txt.at[:, y, :, cols(q)], yn_s.at[k], yn_r.at[y], dev(x, (y + k) % 4, z, c)))
+
+    def swap_texts(s):
         go(rc(txt_in.at[(1 - h) * 2 + s], text_piece(y, q, s), ex_s.at[s], ex_r.at[s], dev(x, y, (z + 4) % 8, c)))
+
+    go(rc(img_in.at[pl.ds(pl.multiple_of(o * 32, 32), 32)], img.at[zl, rows_here, cols(q)], iz_s.at[0],
+          iz_r.at[2 * z + c], me_o))
+    send_images(1)
+    send_images(7)
+    send_texts()
+    swap_texts(0)
+    send_images(2)
+    send_images(6)
+    swap_texts(1)
     loc_i = pltpu.make_async_copy(
         img_in.at[pl.ds(pl.multiple_of(c * 32, 32), 32)], img.at[zl, rows_here, cols(q)], loc_sem.at[1])
     loc_i.start()
@@ -154,26 +168,36 @@
         got(p, yn_r.at[yy])
         go(rc(p, p, ch_s.at[ky], ch_r.at[yy], me_o))
 
+    def swapped_to_other_core(s):
+        for ky in RING:
+            yy = (y + ky) % 4
+            p = text_piece(yy, qp, s)
+            got(p, ye_r.at[2 * yy + s])
+            go(rc(p, p, ch_s.at[4 + 2 * ky + s], ch_r.at[4 + 2 * yy + s], me_o))
+
     along_x(0)
     along_x(1)
     along_x(7)
     pass_on(0)
+    forward_swapped(0)
     along_x(2)
     along_x(6)
-    forward_swapped(0)
     pass_on(1)
     pass_on(7)
+    forward_swapped(1)
     along_x(3)
     along_x(5)
-    forward_swapped(1)
     pass_on(2)
     pass_on(6)
     along_x(4)
-    for k in RING:
-        to_other_core(k)
+    to_other_core(1)
+    to_other_core(3)
+    to_other_core(2)
     pass_on(3)
     pass_on(5)
     pass_on(4)
+    swapped_to_other_core(0)
+    swapped_to_other_core(1)
 
     asum = aps[x]
     for k in RING:
@@ -184,12 +208,6 @@
     for kx in RING:
         go(rc(ap.at[zl], aps.at[x], aps_s.at[kx], aps_r.at[x], dev((x + kx) % 4, y, z, c)))
 
-    for s in (0, 1):
-        for ky in RING:
-            yy = (y + ky) % 4
-            p = text_piece(yy, qp, s)
-            got(p, ye_r.at[2 * yy + s])
-            go(rc(p, p, ch_s.at[4 + 2 * ky + s], ch_r.at[4 + 2 * yy + s], me_o))
     loc_t.wait()
     tsum = tp[y]
     for ky in RING:
@@ -211,15 +229,17 @@
             got(text_piece(yy, 2 * (1 - h) + o, s), ch_r.at[4 + 2 * yy + s])
 
     texts = txt[...].reshape(768, 4 * W)
-    for zz in range(8):
-        for e in (0, 1):
-            got(piece((x + 2) % 4, zz, 16 * e, 16), fw_r.at[2 * zz + e])
-    for half in (0, 1):
+
+    def scores(half):
+        if half == 0:
+            for zz in range(8):
+                for e in (0, 1):
+                    got(piece((x + 2) % 4, zz, 16 * e, 16), fw_r.at[2 * zz + e])
         a = jnp.concatenate(
             [gi_own[0, pl.ds(xx * 128 + zz * 32, 32), 0:128] for zz in (2 * half, 2 * half + 1) for xx in range(4)], axis=0)
         i = img[2 * half : 2 * half + 2].reshape(256, 4 * W)
-        s = lax.dot_general(i, texts, (((1,), (1,)), ((), ())), preferred_element_type=F32)
-        p = jnp.exp(s * INV_TEMP + jnp.concatenate([a] * 6, axis=1) + b).astype(BF16)
+        t = lax.dot_general(i, texts, (((1,), (1,)), ((), ())), preferred_element_type=F32)
+        p = jnp.exp(t * INV_TEMP + jnp.concatenate([a] * 6, axis=1) + b).astype(BF16)
         plan[2 * half : 2 * half + 2] = p.reshape(2, 128, 768)
 
     def own_rows(j, k, e, n=16):
@@ -273,7 +293,7 @@
                 gz_send[j, 16 * e : 16 * e + 16] = t.astype(BF16)
             else:
                 gi_own[0, 16 * e : 16 * e + 16] = t
-        for dz in ((0, 4), (1, 5), (7, 3), (2, 6))[j]:
+        for dz in PAIRS[j]:
             zz = (z + dz) % 8
             both = cols(2 * (zz // 4), 2 * W)
             if dz == 4:
@@ -316,21 +336,23 @@
             go(rc(gf_send.at[1, :, cols(o)], part, gf_s.at[2], gf_r.at[h * 2 + c], me_o))
             gf[h * 2 + c] = gf_send[1, :, cols(c)]
 
+    scores(0)
+    scores(1)
+    text_other(0)
     image_terms(0)
-    text_other(0)
+    text_own(0)
     image_terms(1)
-    text_own(0)
+    text_other(1)
+    image_relay(0)
+    text_own(1)
     image_terms(2)
-    text_other(1)
+    image_relay(1)
     image_terms(3)
-    text_own(1)
-    image_relay(0)
-    image_relay(1)
     image_relay(2)
+    image_sums(0)
+    text_sums(0)
+    image_sums(1)
     image_relay(3)
-    image_sums(0)
-    image_sums(1)
-    text_sums(0)
     image_sums(2)
     image_sums(3)
     text_sums(1)
@@ -354,6 +376,7 @@
 
 
 def on_device(images, texts, image_potential, text_potential):
+    given = (images, texts.reshape(4, 96, W), image_potential, text_potential)
     dma = pltpu.SemaphoreType.DMA
     vm = pltpu.VMEM
     hbm = pl.BlockSpec(memory_space=pltpu.HBM)
@@ -376,10 +399,10 @@
             dma((24,)), dma((24,)), dma((16,)), dma((16,)), dma((4,)), dma((4,)), dma((2,)), dma((2,)), dma((8,)), dma((8,)), dma((4,)), dma((4,)),
         ],
         compiler_params=pltpu.CompilerParams(
-            collective_id=0, has_side_effects=True, vmem_limit_bytes=63 * 1024 * 1024
+            collective_id=0, has_side_effects=True, vmem_limit_bytes=48 * 1024 * 1024
         ),
         cost_estimate=pl.CostEstimate(flops=3623878656, bytes_accessed=2000000, transcendentals=393216),
-    )(images, texts.reshape(4, 96, W), image_potential, text_potential)
+    )(*(pltpu.with_memory_space_constraint(v, pltpu.HBM) for v in given))
 
 
 def solution(mesh):

time: 71.6 us -> 67.2 us (0.939)
  Pallas kernels: 67.3 us -> 65 us
  local copies, waits for them, and re-layouts: 3.46 us -> 1.46 us
    pallas_call x1, Pallas kernels: 67.3 us -> 65 us  [on_device(): pl.pallas_call(kernel, out_shape=(jax.ShapeDtypeStruct((64, W), F32), jax...]
    unnamed x2, local copies, waits for them, and re-layouts: 3.46 us -> 1.46 us
where the time goes in v3:
time: 67.2 us; the launch traced here: 67.1 us
  Pallas kernels  65 us (97%)
  local copies, waits for them, and re-layouts  1.46 us (2%)
    pallas_call x1, Pallas kernels, on_device(): pl.pallas_call(kernel, out_shape=(jax.ShapeDtypeStruct((64, W), F32), jax...  65 us
    unnamed x2, local copies, waits for them, and re-layouts  1.46 us

profile of v3, /device:TPU:1, one launch (start us, length us, event | category | flops | bytes accessed | tf_op | source)
XLA Modules:
  0.0 67.1 jit_solution(4658473739910899020)
XLA Ops:
  0.6 65.0 %shard_map.59 = (f32[64,384]{1,0:T(8,128)S(1)}, f32[384,384]{1,0:T(8,128)S(1)}) custom-call(bf16[64,384]{1,0:T(8,128)(2,1)} %img_in.1, bf16[4,96,384]{2,1,0:T(8,128)(2,1)} %bitcast.1, f32[64]{0:T(128)} %ip_in.1, f32[384]{0:T(512)} %tp_in.1), custom_call_target="tpu_custom_call" | custom-call | flops 3623878656 | bytes 2000000 | tf_op jit(solution)/shard_map/pallas_call | solution.py:383
  65.6 0.6 copy.8
  66.3 0.8 %copy.9 = f32[384,384]{1,0:T(8,128)} copy(f32[384,384]{1,0:T(8,128)S(1)} %get-tuple-element.5) | data formatting | bytes 1179648

commit v4 on v3

--- a/solution.py
+++ b/solution.py
@@ -12,6 +12,7 @@
 ZORDER = (1, 7, 2, 6, 4)
 RING = (1, 3, 2)
 ORDER = (0, 1, 3, 2)
+DIRECT = (4,)
 PAIRS = ((0, 4), (1, 5), (7, 3), (2, 6))
 W = 384
 
@@ -107,8 +108,8 @@
           iz_r.at[2 * z + c], me_o))
     send_images(1)
     send_images(7)
+    swap_texts(0)
     send_texts()
-    swap_texts(0)
     send_images(2)
     send_images(6)
     swap_texts(1)
@@ -131,6 +132,8 @@
         for e, kx in ((0, 1), (1, 3)):
             back = (x + 4 - kx) % 4
             got(piece(back, zz), ix_r.at[8 * back + zz])
+            if k in DIRECT:
+                continue
             half = piece(back, zz, 16 * e, 16)
             go(rc(half, half, fw_s.at[2 * k + e], fw_r.at[2 * zz + e], dev((x + kx) % 4, y, z, c)))
 
@@ -154,6 +157,10 @@
             go(rc(p, p, iz_s.at[7 + 2 * e], iz_r.at[2 * zz + e], dev(x, y, (z + 2 * step) % 8, c)))
         for e, kx in ((0, 1), (1, 3)):
             go(rc(piece(x, zz), piece(x, zz), ix_s.at[2 * k + e], ix_r.at[8 * x + zz], dev((x + kx) % 4, y, z, c)))
+        if k in DIRECT:
+            for e in (0, 1):
+                p = piece(x, zz, 16 * e, 16)
+                go(rc(p, p, fw_s.at[2 * k + e], fw_r.at[2 * zz + e], dev((x + 2) % 4, y, z, c)))
 
     def forward_swapped(s):
         p = text_piece(y, qp, s)
@@ -174,6 +181,16 @@
             p = text_piece(yy, qp, s)
             got(p, ye_r.at[2 * yy + s])
             go(rc(p, p, ch_s.at[4 + 2 * ky + s], ch_r.at[4 + 2 * yy + s], me_o))
+
+    def potentials(_):
+        asum = aps[x]
+        for k in RING:
+            zz = (zl + k) % 4
+            got(ap.at[zz], ap_r.at[zz])
+            asum = asum + ap[zz]
+        ap[zl] = asum
+        for kx in RING:
+            go(rc(ap.at[zl], aps.at[x], aps_s.at[kx], aps_r.at[x], dev((x + kx) % 4, y, z, c)))
 
     along_x(0)
     along_x(1)
@@ -182,6 +199,7 @@
     forward_swapped(0)
     along_x(2)
     along_x(6)
+    potentials(0)
     pass_on(1)
     pass_on(7)
     forward_swapped(1)
@@ -199,15 +217,6 @@
     swapped_to_other_core(0)
     swapped_to_other_core(1)
 
-    asum = aps[x]
-    for k in RING:
-        zz = (zl + k) % 4
-        got(ap.at[zz], ap_r.at[zz])
-        asum = asum + ap[zz]
-    ap[zl] = asum
-    for kx in RING:
-        go(rc(ap.at[zl], aps.at[x], aps_s.at[kx], aps_r.at[x], dev((x + kx) % 4, y, z, c)))
-
     loc_t.wait()
     tsum = tp[y]
     for ky in RING:
@@ -215,7 +224,7 @@
         got(tp.at[yy], tp_r.at[yy])
         tsum = tsum + tp[yy]
     b = tsum[0:1]
-    a_of = {0: jnp.broadcast_to(asum[0:1], (128, 128)).T}
+    a_of = {0: jnp.broadcast_to(ap[zl][0:1], (128, 128)).T}
     for kx in RING:
         xx = (x + kx) % 4
         got(aps.at[xx], aps_r.at[xx])

time: 67.2 us -> 65.5 us (0.975)
  Pallas kernels: 65 us -> 63.2 us
    pallas_call x1, Pallas kernels: 65 us -> 63.2 us  [on_device(): pl.pallas_call(kernel, out_shape=(jax.ShapeDtypeStruct((64, W), F32), jax...]
where the time goes in v4:
time: 65.5 us; the launch traced here: 65.3 us
  Pallas kernels  63.2 us (96%)
  local copies, waits for them, and re-layouts  1.46 us (2%)
    pallas_call x1, Pallas kernels, on_device(): pl.pallas_call(kernel, out_shape=(jax.ShapeDtypeStruct((64, W), F32), jax...  63.2 us
    unnamed x2, local copies, waits for them, and re-layouts  1.46 us

profile of v4, /device:TPU:1, one launch (start us, length us, event | category | flops | bytes accessed | tf_op | source)
XLA Modules:
  0.0 65.3 jit_solution(14794576908328362906)
XLA Ops:
  0.6 63.2 %shard_map.59 = (f32[64,384]{1,0:T(8,128)S(1)}, f32[384,384]{1,0:T(8,128)S(1)}) custom-call(bf16[64,384]{1,0:T(8,128)(2,1)} %img_in.1, bf16[4,96,384]{2,1,0:T(8,128)(2,1)} %bitcast.1, f32[64]{0:T(128)} %ip_in.1, f32[384]{0:T(512)} %tp_in.1), custom_call_target="tpu_custom_call" | custom-call | flops 3623878656 | bytes 2000000 | tf_op jit(solution)/shard_map/pallas_call | solution.py:392
  63.9 0.6 copy.8
  64.5 0.8 %copy.9 = f32[384,384]{1,0:T(8,128)} copy(f32[384,384]{1,0:T(8,128)S(1)} %get-tuple-element.5) | data formatting | bytes 1179648

commit v5 on v4

--- a/solution.py
+++ b/solution.py
@@ -366,22 +366,22 @@
     image_sums(3)
     text_sums(1)
 
+    for dd in (h * 2 + o, (1 - h) * 2, (1 - h) * 2 + 1):
+        got(gf.at[dd], gf_r.at[dd])
+    for dd in range(4):
+        gt_out[dd * 96 : (dd + 1) * 96] = gf[dd].astype(F32)
+    for cp in sends:
+        cp.wait_send()
     for k in (1, 7, 2, 6):
         zz = (z + k) % 8
         for cc in (0, 1):
             got(gz.at[zz, cc], gz_r.at[2 * zz + cc])
     got(gz.at[z, o], gz_r.at[2 * z + o])
-    for dd in (h * 2 + o, (1 - h) * 2, (1 - h) * 2 + 1):
-        got(gf.at[dd], gf_r.at[dd])
     for r in (0, 1):
         t = gz[z, r].astype(F32)
         for k in (1, 7, 2, 6):
             t = t + gz[(z + k) % 8, r].astype(F32)
         gi_out[r * 32 : (r + 1) * 32] = t
-    for dd in range(4):
-        gt_out[dd * 96 : (dd + 1) * 96] = gf[dd].astype(F32)
-    for cp in sends:
-        cp.wait_send()
 
 
 def on_device(images, texts, image_potential, text_potential):

time: 65.5 us -> 65.2 us (level)
  no operation moved by 1% of the time
where the time goes in v5:
time: 65.2 us; the launch traced here: 65.1 us
  Pallas kernels  63 us (97%)
  local copies, waits for them, and re-layouts  1.46 us (2%)
    pallas_call x1, Pallas kernels, on_device(): pl.pallas_call(kernel, out_shape=(jax.ShapeDtypeStruct((64, W), F32), jax...  63 us
    unnamed x2, local copies, waits for them, and re-layouts  1.46 us

profile of v5, /device:TPU:1, one launch (start us, length us, event | category | flops | bytes accessed | tf_op | source)
XLA Modules:
  0.0 65.1 jit_solution(14125562132275299574)
XLA Ops:
  0.6 63.0 %shard_map.59 = (f32[64,384]{1,0:T(8,128)S(1)}, f32[384,384]{1,0:T(8,128)S(1)}) custom-call(bf16[64,384]{1,0:T(8,128)(2,1)} %img_in.1, bf16[4,96,384]{2,1,0:T(8,128)(2,1)} %bitcast.1, f32[64]{0:T(128)} %ip_in.1, f32[384]{0:T(512)} %tp_in.1), custom_call_target="tpu_custom_call" | custom-call | flops 3623878656 | bytes 2000000 | tf_op jit(solution)/shard_map/pallas_call | solution.py:392
  63.6 0.6 copy.8
  64.3 0.8 %copy.9 = f32[384,384]{1,0:T(8,128)} copy(f32[384,384]{1,0:T(8,128)S(1)} %get-tuple-element.5) | data formatting | bytes 1179648
